TPU v7x, 32 devices: a whole 2x2x4 slice. The times are simulated.
32 devices in a mesh: dp: 16 (over z, x, core), head: 2 (over y).
Axes of the slice: x: 2, y: 2, z: 4, core: 2. Of those that a mesh axis runs over, the one named last changes fastest.
Arguments:
- stream_x: bfloat16 [32768, 512], P(('dp', 'head')), may hold values from -6 to 6
- stream_y: bfloat16 [32768, 512], P(('dp', 'head')), may hold values from -6 to 6
- segments: int32 [32768], P('dp'), may hold values from 0 to 8, as said below
- keep_mask: int32 [32768], P('dp'), may hold values 0 or 1
- query_weight: bfloat16 [512, 512], P(None, 'head'), may hold values from -0.25 to 0.25
- key_weight: bfloat16 [512, 512], P(None, 'head'), may hold values from -0.25 to 0.25
- value_weight: bfloat16 [512, 512], P(None, 'head'), may hold values from -0.25 to 0.25
- output_weight: bfloat16 [512, 512], P('head'), may hold values from -1.5 to 1.5
- first_gain: float32 [512], replicated, may hold values from 0.5 to 1.5
- first_shift: float32 [512], replicated, may hold values from -2 to 2
- up_weight: bfloat16 [2048, 512], P(('dp', 'head')), may hold values from -0.25 to 0.25
- down_weight: bfloat16 [2048, 512], P(('dp', 'head')), may hold values from -0.125 to 0.125
- second_gain: float32 [512], replicated, may hold values from 0.5 to 1.5
- second_shift: float32 [512], replicated, may hold values from -2 to 2
- grad_stream: bfloat16 [32768, 512], P(('dp', 'head')), may hold values from -6 to 6
- grad_dual: bfloat16 [32768, 512], P(('dp', 'head')), may hold values from -6 to 6
Outputs:
- new_stream: bfloat16 [32768, 512], P(('dp', 'head'))
- new_dual: bfloat16 [32768, 512], P(('dp', 'head'))
- stream_grad: float32 [32768, 512], P(('dp', 'head'))
- query_grad: float32 [512, 512], P(None, 'head')
- key_grad: float32 [512, 512], P(None, 'head')
- value_grad: float32 [512, 512], P(None, 'head')
- output_grad: float32 [512, 512], P('head')
- first_gain_grad: float32 [512], replicated
- first_shift_grad: float32 [512], replicated
- up_grad: float32 [2048, 512], P(('dp', 'head'))
- down_grad: float32 [2048, 512], P(('dp', 'head'))
- second_gain_grad: float32 [512], replicated
- second_shift_grad: float32 [512], replicated
Inputs may be any that keep to these rules, and one draw needn't show every extreme that they name: `segments`: within each sequence of 1024 tokens the ids never fall; equal ids mark one document. Each sequence begins with id 0 and ends with the largest id.
All inputs are finite; a program needn't handle non-finite values. No bound on the sum of `keep_mask` on one device may be relied on, other than what follows from the above.
Results may differ from a plain program's by a relative error of at most 0.018.
Values may be sent and summed in bfloat16 or wider, within the bound.
No kernel may reach another device: no remote copies, remote signals or barrier semaphores. Data moves between devices by JAX's collectives and lax.ppermute only.
A program may use at most 128 MiB of HBM per device.

v0:
```python
import math

import jax
import jax.numpy as jnp
from jax import lax
from jax.sharding import PartitionSpec as P

HEADS = 8
SEQ = 1024


epsilon = 1e-05


def norm_forward(values, gain_vec, shift_vec):
    row_mean = jnp.mean(values, axis=-1, keepdims=True)
    centred = values - row_mean
    variance = jnp.mean(centred * centred, axis=-1, keepdims=True)
    return centred * lax.rsqrt(variance + epsilon) * gain_vec + shift_vec


def exact_gelu(values):
    return jax.nn.gelu(values, approximate=False)


def allowed_mask(offset, length, seg_ids, keep_ids):
    query_pos = offset + lax.iota(jnp.int32, length)
    key_pos = lax.iota(jnp.int32, seg_ids.shape[0])
    query_seg = lax.dynamic_slice_in_dim(seg_ids, offset, length)
    same_doc = query_seg[:, None] == seg_ids[None, :]
    causal = key_pos[None, :] <= query_pos[:, None]
    visible = (keep_ids[None, :] == 1) | (key_pos[None, :] == query_pos[:, None])
    return same_doc & causal & visible


def masked_scores(query_block, key_rows, offset, seg_ids, keep_ids, score_scale):
    scores = (
        jnp.einsum("hqd,hkd->hqk", query_block, key_rows, preferred_element_type=jnp.float32)
        * score_scale
    )
    allowed = allowed_mask(offset, query_block.shape[1], seg_ids, keep_ids)[None]
    return jnp.where(allowed, scores, -1e30)


def split_heads(matrix, head_dim):
    return matrix.reshape(matrix.shape[0], -1, head_dim).transpose(1, 0, 2)


def join_blocks(stacked):
    return stacked.transpose(0, 2, 1, 3).reshape(
        stacked.shape[0] * stacked.shape[2], stacked.shape[1] * stacked.shape[3]
    )


def join_heads(stacked):
    return stacked.transpose(1, 0, 2).reshape(stacked.shape[1], stacked.shape[0] * stacked.shape[2])


def block_context(block_index, block_len, seq_len):
    offset = block_index * block_len
    seq_start = offset // seq_len * seq_len
    return (offset, seq_start, offset - seq_start)


def attention_forward(queries, key_rows, value_rows, seg_ids, keep_ids, score_scale, seq_len):
    group_tokens = key_rows.shape[1]
    block_len = min(512, seq_len)

    def one_block(block_index):
        offset, seq_start, inner_off = block_context(block_index, block_len, seq_len)
        query_block = lax.dynamic_slice_in_dim(queries, offset, block_len, 1)
        seq_keys = lax.dynamic_slice_in_dim(key_rows, seq_start, seq_len, 1)
        seq_values = lax.dynamic_slice_in_dim(value_rows, seq_start, seq_len, 1)
        seq_segs = lax.dynamic_slice_in_dim(seg_ids, seq_start, seq_len)
        seq_keep = lax.dynamic_slice_in_dim(keep_ids, seq_start, seq_len)
        scores = masked_scores(query_block, seq_keys, inner_off, seq_segs, seq_keep, score_scale)
        row_max = jnp.max(scores, axis=-1, keepdims=True)
        exp_terms = jnp.exp(scores - row_max)
        row_sum = jnp.sum(exp_terms, axis=-1, keepdims=True)
        probability = (exp_terms / row_sum).astype(jnp.bfloat16)
        attended = jnp.einsum(
            "hqk,hkd->hqd", probability, seq_values, preferred_element_type=jnp.float32
        ).astype(jnp.bfloat16)
        return (attended, row_max[..., 0] + jnp.log(row_sum[..., 0]))

    return lax.map(one_block, jnp.arange(group_tokens // block_len, dtype=jnp.int32))


def attention_backward(
    queries, key_rows, value_rows, log_total, grad_attended, seg_ids, keep_ids, score_scale, seq_len
):
    group_tokens = key_rows.shape[1]
    block_len = min(512, seq_len)

    def one_block(running, items):
        key_acc, value_acc = running
        block_index, block_total = items
        offset, seq_start, inner_off = block_context(block_index, block_len, seq_len)
        query_block = lax.dynamic_slice_in_dim(queries, offset, block_len, 1)
        grad_block = lax.dynamic_slice_in_dim(grad_attended, offset, block_len, 1)
        seq_keys = lax.dynamic_slice_in_dim(key_rows, seq_start, seq_len, 1)
        seq_values = lax.dynamic_slice_in_dim(value_rows, seq_start, seq_len, 1)
        seq_segs = lax.dynamic_slice_in_dim(seg_ids, seq_start, seq_len)
        seq_keep = lax.dynamic_slice_in_dim(keep_ids, seq_start, seq_len)
        scores = masked_scores(query_block, seq_keys, inner_off, seq_segs, seq_keep, score_scale)
        probability = jnp.exp(scores - block_total[..., None])
        grad_prob = jnp.einsum(
            "hqd,hkd->hqk", grad_block, seq_values, preferred_element_type=jnp.float32
        )
        inner = jnp.sum(probability * grad_prob, axis=-1, keepdims=True)
        grad_scores = (probability * (grad_prob - inner)).astype(jnp.bfloat16)
        query_grad = (
            jnp.einsum("hqk,hkd->hqd", grad_scores, seq_keys, preferred_element_type=jnp.float32)
            * score_scale
        )
        key_part = (
            jnp.einsum("hqk,hqd->hkd", grad_scores, query_block, preferred_element_type=jnp.float32)
            * score_scale
        )
        value_part = jnp.einsum(
            "hqk,hqd->hkd",
            probability.astype(jnp.bfloat16),
            grad_block,
            preferred_element_type=jnp.float32,
        )
        key_now = lax.dynamic_slice_in_dim(key_acc, seq_start, seq_len, 1)
        value_now = lax.dynamic_slice_in_dim(value_acc, seq_start, seq_len, 1)
        key_acc = lax.dynamic_update_slice_in_dim(key_acc, key_now + key_part, seq_start, 1)
        value_acc = lax.dynamic_update_slice_in_dim(value_acc, value_now + value_part, seq_start, 1)
        return ((key_acc, value_acc), query_grad)

    empty = jnp.zeros(key_rows.shape, jnp.float32)
    indices = jnp.arange(group_tokens // block_len, dtype=jnp.int32)
    (key_acc, value_acc), query_grad = lax.scan(one_block, (empty, empty), (indices, log_total))
    return (query_grad, key_acc, value_acc)


def body(
    stream_x,
    stream_y,
    segments,
    keep_mask,
    query_weight,
    key_weight,
    value_weight,
    output_weight,
    first_gain,
    first_shift,
    up_weight,
    down_weight,
    second_gain,
    second_shift,
    grad_stream,
    grad_dual,
):
    row_count, model_width = stream_x.shape
    heads_cols = query_weight.shape[1]
    head_dim = model_width // HEADS
    seq_len = SEQ
    score_scale = 1.0 / math.sqrt(head_dim)
    contract_cols = (((1,), (1,)), ((), ()))
    contract_rows = (((0,), (0,)), ((), ()))
    proj_local = jnp.concatenate([query_weight, key_weight, value_weight], axis=1)
    gathered = lax.all_gather(stream_x, "head", axis=0, tiled=True)
    packed = jnp.dot(gathered, proj_local, preferred_element_type=jnp.float32).astype(jnp.bfloat16)
    queries = split_heads(packed[:, :heads_cols], head_dim)
    key_rows = split_heads(packed[:, heads_cols : 2 * heads_cols], head_dim)
    value_rows = split_heads(packed[:, 2 * heads_cols :], head_dim)
    attended_blocks, log_total = attention_forward(
        queries, key_rows, value_rows, segments, keep_mask, score_scale, seq_len
    )
    merged = join_blocks(attended_blocks)
    window = merged
    branch = lax.psum_scatter(
        jnp.dot(window, output_weight, preferred_element_type=jnp.float32),
        "head",
        scatter_dimension=0,
        tiled=True,
    )
    mixed = stream_x.astype(jnp.float32) + branch
    first_out = norm_forward(mixed, first_gain, first_shift)
    first_low = first_out.astype(jnp.bfloat16)
    up_whole, down_whole = (
        lax.all_gather(up_weight, ("dp", "head"), axis=0, tiled=True),
        lax.all_gather(down_weight, ("dp", "head"), axis=0, tiled=True),
    )
    hidden = lax.dot_general(first_low, up_whole, contract_cols, preferred_element_type=jnp.float32)
    activated = exact_gelu(hidden).astype(jnp.bfloat16)
    ffn_out = jnp.dot(activated, down_whole, preferred_element_type=jnp.float32)
    second_in = first_out + ffn_out
    new_stream = norm_forward(second_in, second_gain, second_shift)
    dual_sum = stream_y.astype(jnp.float32) + branch + ffn_out
    cot_stream = grad_stream.astype(jnp.float32)
    cot_dual = grad_dual.astype(jnp.float32)
    second_values, second_back = jax.vjp(norm_forward, second_in, second_gain, second_shift)
    grad_second, second_gain_part, second_shift_part = second_back(cot_stream)
    grad_ffn = (grad_second + cot_dual).astype(jnp.bfloat16)
    down_part = lax.dot_general(
        activated, grad_ffn, contract_rows, preferred_element_type=jnp.float32
    )
    grad_act = lax.dot_general(
        grad_ffn, down_whole, contract_cols, preferred_element_type=jnp.float32
    )
    gelu_values, gelu_back = jax.vjp(exact_gelu, hidden)
    grad_hidden = gelu_back(grad_act)[0].astype(jnp.bfloat16)
    up_part = lax.dot_general(
        grad_hidden, first_low, contract_rows, preferred_element_type=jnp.float32
    )
    grad_first = grad_second + jnp.dot(grad_hidden, up_whole, preferred_element_type=jnp.float32)
    first_values, first_back = jax.vjp(norm_forward, mixed, first_gain, first_shift)
    grad_mixed, first_gain_part, first_shift_part = first_back(grad_first)
    grad_branch = (grad_mixed + cot_dual).astype(jnp.bfloat16)
    portion = lax.all_gather(grad_branch, "head", axis=0, tiled=True)
    grad_part = lax.dot_general(
        portion, output_weight, contract_cols, preferred_element_type=jnp.float32
    )
    grad_merged = grad_part
    window = merged
    weight_acc = lax.dot_general(window, portion, contract_rows, preferred_element_type=jnp.float32)
    grad_merged, out_weight_part = (grad_merged, weight_acc)
    grad_merged = grad_merged.astype(jnp.bfloat16)
    grad_attended = split_heads(grad_merged, head_dim)
    query_blocks, key_acc, value_acc = attention_backward(
        queries,
        key_rows,
        value_rows,
        log_total,
        grad_attended,
        segments,
        keep_mask,
        score_scale,
        seq_len,
    )
    grad_packed = jnp.concatenate(
        [join_blocks(query_blocks), join_heads(key_acc), join_heads(value_acc)], axis=1
    ).astype(jnp.bfloat16)
    window = grad_packed
    grad_input = lax.psum_scatter(
        lax.dot_general(
            window, proj_local, contract_cols, preferred_element_type=jnp.float32
        ).astype(jnp.bfloat16),
        "head",
        scatter_dimension=0,
        tiled=True,
    ).astype(jnp.float32)
    stream_grad = grad_mixed + grad_input
    proj_part = lax.dot_general(
        gathered, grad_packed, contract_rows, preferred_element_type=jnp.float32
    )
    proj_sum, output_grad = (
        lax.psum(proj_part.astype(jnp.bfloat16), "dp").astype(jnp.float32),
        lax.psum(out_weight_part.astype(jnp.bfloat16), "dp").astype(jnp.float32),
    )
    up_grad, down_grad = (
        lax.psum_scatter(up_part, ("dp", "head"), scatter_dimension=0, tiled=True),
        lax.psum_scatter(down_part, ("dp", "head"), scatter_dimension=0, tiled=True),
    )
    first_gain_grad, first_shift_grad, second_gain_grad, second_shift_grad = lax.psum(
        (first_gain_part, first_shift_part, second_gain_part, second_shift_part), ("dp", "head")
    )
    return (
        new_stream.astype(jnp.bfloat16),
        dual_sum.astype(jnp.bfloat16),
        stream_grad,
        proj_sum[:, :heads_cols],
        proj_sum[:, heads_cols : 2 * heads_cols],
        proj_sum[:, 2 * heads_cols :],
        output_grad,
        first_gain_grad,
        first_shift_grad,
        up_grad,
        down_grad,
        second_gain_grad,
        second_shift_grad,
    )


def solution(mesh):
    in_specs = (
        P(("dp", "head"), None),
        P(("dp", "head"), None),
        P("dp"),
        P("dp"),
        P(None, "head"),
        P(None, "head"),
        P(None, "head"),
        P("head", None),
        P(),
        P(),
        P(("dp", "head"), None),
        P(("dp", "head"), None),
        P(),
        P(),
        P(("dp", "head"), None),
        P(("dp", "head"), None),
    )
    out_specs = (
        P(("dp", "head"), None),
        P(("dp", "head"), None),
        P(("dp", "head"), None),
        P(None, "head"),
        P(None, "head"),
        P(None, "head"),
        P("head", None),
        P(),
        P(),
        P(("dp", "head"), None),
        P(("dp", "head"), None),
        P(),
        P(),
    )
    return jax.shard_map(body, mesh=mesh, in_specs=in_specs, out_specs=out_specs, check_vma=False)
```

profile of v0, /device:TPU:0, one launch (start us, length us, event | category | flops | bytes accessed | tf_op | source)
XLA Modules:
  0.0 759.1 jit_solution(3592406584015609243)
XLA Ops:
  11.8 34.5 %all-gather.5.cloned.1.call-done = bf16[2048,512]{1,0:T(8,128)(2,1)} async-done(((bf16[1024,512]{1,0:T(8,128)(2,1)}), bf16[2048,512]{1,0:T(8,128)(2,1)}) %all-gather.5.cloned.1.call-update) | async-done | bytes 2097168 | tf_op jit(solution)/shard_map/all_gather | solution.py:164
  51.1 38.3 %while.30 = (s32[]{:T(128)}, bf16[4,4,512,64]{2,3,1,0:T(8,128)(2,1)}, f32[4,4,512]{2,1,0:T(4,128)S(1)}, s32[4]{0:T(128)S(1)}, s32[2048]{0:T(1024)S(1)}, /*index=...) while((s32[]{:T(128)}, ...), condition=%wide.region_3.4_spmd, body=%wide.region_0.3_spmd.sunk | while | flops 565313024 | bytes 33125424 | solution.py:86
  97.1 53.9 %reduce-scatter.5.cloned.1.call-done = f32[1024,512]{1,0:T(8,128)} async-done(((f32[2048,512]{1,0:T(8,128)}), f32[1024,512]{1,0:T(8,128)}) %reduce-scatter.5.cloned.1.call-update) | async-done | bytes 2097168 | tf_op jit(solution)/shard_map/reduce_scatter | solution.py:174
  153.6 24.7 %all-gather.7.cloned.1.call-done = bf16[2048,512]{1,0:T(8,128)(2,1)} async-done(((bf16[64,512]{1,0:T(8,128)(2,1)}), bf16[2048,512]{1,0:T(8,128)(2,1)}) %all-gather.7.cloned.1.call-update) | async-done | bytes 2097168 | tf_op jit(solution)/shard_map/all_gather | solution.py:184
  178.3 23.9 %multiply_convert_fusion.1 = (bf16[1024,2048]{1,0:T(8,128)(2,1)}, f32[1024,2048]{1,0:T(8,128)}, f32[1024,2048]{1,0:T(8,128)}) fusion(bf16[2048,512]{1,0:T(8,128)(2,1)} %all-gather.7.cloned.1.call-done, f32[1024,512]{1,0:T(8,128)S(1)} %get-tuple-element.374, f32[512]{0:T(512)S(1)} %copy-done.31, f32[512]{0:T(512)S(1)} %copy-done.26, f32[1024]{0:T(1024)S(1)} %fusion.66, ...), kind=kOutput, calls=%fused_computation.66 | convolution fusion | flops 2286419968 | bytes 25178112 | tf_op jit(solution)/shard_map/dot_general | solution.py:187
  202.3 35.0 %all-gather.9.cloned.1.call-done = bf16[2048,512]{1,0:T(8,128)(2,1)} async-done(((bf16[64,512]{1,0:T(8,128)(2,1)}), bf16[2048,512]{1,0:T(8,128)(2,1)}) %all-gather.9.cloned.1.call-update) | async-done | bytes 2097168 | tf_op jit(solution)/shard_map/all_gather | solution.py:185
  237.2 7.5 fusion.76
  251.4 17.2 %add_convert_fusion = bf16[1024,2048]{1,0:T(8,128)(2,1)S(1)} fusion(f32[1024,2048]{1,0:T(8,128)S(1)} %copy-done.34, f32[1024,2048]{1,0:T(8,128)} %get-tuple-element.387, bf16[1024,512]{1,0:T(8,128)(2,1)S(1)} %fusion.60, bf16[2048,512]{1,0:T(8,128)(2,1)S(1)} %copy-done.30), kind=kOutput, calls=%fused_computation.65 | convolution fusion | flops 2176843776 | bytes 24117248 | tf_op jit(solution)/shard_map/dot_general | solution.py:201
  275.2 32.1 %all-gather.11.cloned.1.call-done = bf16[2048,512]{1,0:T(8,128)(2,1)} async-done(((bf16[1024,512]{1,0:T(8,128)(2,1)}), bf16[2048,512]{1,0:T(8,128)(2,1)}) %all-gather.11.cloned.1.call-update) | async-done | bytes 2097168 | tf_op jit(solution)/shard_map/all_gather | solution.py:213
  312.4 105.2 %while.31 = (s32[]{:T(128)}, f32[4,2048,64]{1,2,0:T(8,128)S(1)}, f32[4,2048,64]{1,2,0:T(8,128)}, bf16[4,4,512,64]{2,3,1,0:T(8,128)(2,1)}, s32[4]{0:T(128)S(1)}, ...) while((s32[]{:T(128)}, f32[4,2048,64]{1,2,0:T(8,128)S(1)}, ...), condition=%wide.region_15.16_spmd, body=%wide.region_13.15_spmd.sunk | while | flops 1377697280 | bytes 105992872 | solution.py:134
  313.7 5.5 fusion.137
  320.2 6.9 multiply_reduce_fusion.6
  339.9 5.5 fusion.137
  346.4 6.9 multiply_reduce_fusion.6
  366.2 5.5 fusion.137
  372.7 6.9 multiply_reduce_fusion.6
  392.4 5.5 fusion.137
  398.9 6.9 multiply_reduce_fusion.6
  432.0 6.8 fusion.83
  440.4 6.7 fusion.70
  447.8 40.4 %all-reduce = (f32[512]{0:T(512)}, f32[512]{0:T(512)}, f32[512]{0:T(512)}, f32[512]{0:T(512)}) all-reduce(f32[512]{0:T(512)S(1)} %get-tuple-element.311, f32[512]{0:T(512)S(1)} %get-tuple-element.315, f32[512]{0:T(512)S(1)} %copy-done.23, f32[512]{0:T(512)S(1)} %copy-done.24), channel_id=1, replica_groups=mesh['dp'=16,'head'=2] {'dp','head'}, use_global_device_ids=true, to_apply=%region_20.21 | all-reduce | flops 2048 | bytes 16384 | tf_op jit(solution)/shard_map/psum | solution.py:258
  488.2 32.5 %all-reduce.4.cloned.1.call-done = (bf16[512,768]{0,1:T(8,128)(2,1)}, bf16[256,512]{1,0:T(8,128)(2,1)}) async-done(((bf16[512,768]{0,1:T(8,128)(2,1)}, bf16[256,512]{1,0:T(8,128)(2,1)}), (bf16[512,768]{0,1:T(8,128)(2,1)}, bf16[256,512]{1,0:T(8,128)(2,1)})) %all-reduce.4.cloned.1.call-update) | async-done | bytes 1048592 | tf_op jit(solution)/shard_map/psum | solution.py:251
  531.5 78.2 %reduce-scatter.11.cloned.1.call-done = f32[64,512]{1,0:T(8,128)} async-done(((f32[2048,512]{1,0:T(8,128)}), f32[64,512]{1,0:T(8,128)}) %reduce-scatter.11.cloned.1.call-update) | async-done | bytes 131088 | tf_op jit(solution)/shard_map/reduce_scatter | solution.py:256
  609.7 141.4 %reduce-scatter.9.cloned.1.call-done = f32[64,512]{1,0:T(8,128)} async-done(((f32[2048,512]{1,0:T(8,128)}), f32[64,512]{1,0:T(8,128)}) %reduce-scatter.9.cloned.1.call-update) | async-done | bytes 131088 | tf_op jit(solution)/shard_map/reduce_scatter | solution.py:255
  (257 shorter events, 152.1 us)
Async XLA Ops:
  8.0 85.1 %copy-start = (bf16[256,512]{1,0:T(8,128)(2,1)S(1)}, bf16[256,512]{1,0:T(8,128)(2,1)}, u32[]{:S(2)}) copy-start(bf16[256,512]{1,0:T(8,128)(2,1)} %param.27) | copy-start | bytes 786436
  8.0 38.2 %all-gather.5.cloned.1.call-start = ((), (), s32[]{:S(2)}) async-start(), calls=%async_computation.4 | async-start | bytes 3145728 | tf_op jit(solution)/shard_map/all_gather | solution.py:164
  8.8 142.2 %reduce-scatter.5.cloned.1.call-start = ((), (), s32[]{:S(2)}) async-start(), calls=%async_computation.5 | async-start | bytes 6291456 | tf_op jit(solution)/shard_map/reduce_scatter | solution.py:174
  11.7 34.5 %copy-start.20 = (bf16[512,768]{1,0:T(8,128)(2,1)}, bf16[512,768]{1,0:T(8,128)(2,1)S(1)}, u32[]{:S(2)}) copy-start(bf16[512,768]{1,0:T(8,128)(2,1)S(1)} %constant_dynamic-update-slice_fusion) | copy-start | bytes 2359300
  95.8 82.5 %copy-start.26 = (f32[512]{0:T(512)S(1)}, f32[512]{0:T(512)}, u32[]{:S(2)}) copy-start(f32[512]{0:T(512)} %param.28) | copy-start | bytes 6148
  95.8 82.5 %copy-start.31 = (f32[512]{0:T(512)S(1)}, f32[512]{0:T(512)}, u32[]{:S(2)}) copy-start(f32[512]{0:T(512)} %param.29) | copy-start | bytes 6148
  95.9 82.5 %all-gather.7.cloned.1.call-start = ((), (), s32[]{:S(2)}) async-start(), calls=%async_computation.6 | async-start | bytes 2162688 | tf_op jit(solution)/shard_map/all_gather | solution.py:184
  96.4 140.8 %all-gather.9.cloned.1.call-start = ((), (), s32[]{:S(2)}) async-start(), calls=%async_computation.7 | async-start | bytes 2162688 | tf_op jit(solution)/shard_map/all_gather | solution.py:185
  97.0 210.3 %all-gather.11.cloned.1.call-start = ((), (), s32[]{:S(2)}) async-start(), calls=%async_computation.8 | async-start | bytes 3145728 | tf_op jit(solution)/shard_map/all_gather | solution.py:213
  153.1 118.4 %copy-start.5 = (f32[1024,512]{1,0:T(8,128)}, f32[1024,512]{1,0:T(8,128)S(1)}, u32[]{:S(2)}) copy-start(f32[1024,512]{1,0:T(8,128)S(1)} %get-tuple-element.374) | copy-start | bytes 6291460
  237.2 7.9 %copy-start.11 = (bf16[1024,512]{1,0:T(8,128)(2,1)S(1)}, bf16[1024,512]{1,0:T(8,128)(2,1)}, u32[]{:S(2)}) copy-start(bf16[1024,512]{1,0:T(8,128)(2,1)} %param.34) | copy-start | bytes 3145732
  237.2 7.9 %copy-start.22 = (f32[512]{0:T(512)S(1)}, f32[512]{0:T(512)}, u32[]{:S(2)}) copy-start(f32[512]{0:T(512)} %param.32) | copy-start | bytes 6148
  248.9 19.7 %copy-start.12 = (bf16[1024,512]{1,0:T(8,128)(2,1)}, bf16[1024,512]{1,0:T(8,128)(2,1)S(1)}, u32[]{:S(2)}) copy-start(bf16[1024,512]{1,0:T(8,128)(2,1)S(1)} %fusion.60) | copy-start | bytes 3145732
  251.4 17.2 %copy-start.29 = (bf16[2048,512]{1,0:T(8,128)(2,1)S(1)}, bf16[2048,512]{1,0:T(8,128)(2,1)}, u32[]{:S(2)}) copy-start(bf16[2048,512]{1,0:T(8,128)(2,1)} %all-gather.7.cloned.1.call-done) | copy-start | bytes 6291460
  275.1 245.5 %all-reduce.4.cloned.1.call-start = ((), (), s32[]{:S(2)}) async-start(), calls=%async_computation.12 | async-start | bytes 2097152 | tf_op jit(solution)/shard_map/psum | solution.py:251
  320.1 6.9 slice-start
  320.2 6.9 slice-start.1
  346.4 6.9 slice-start
  372.6 6.9 slice-start
  427.1 101.6 %reduce-scatter.7.cloned.1.call-start = ((), (), s32[]{:S(2)}) async-start(), calls=%async_computation.9 | async-start | bytes 3145728 | tf_op jit(solution)/shard_map/reduce_scatter | solution.py:238
  432.0 177.7 %reduce-scatter.11.cloned.1.call-start = ((), (), s32[]{:S(2)}) async-start(), calls=%async_computation.11 | async-start | bytes 4325376 | tf_op jit(solution)/shard_map/reduce_scatter | solution.py:256
  438.8 312.3 %reduce-scatter.9.cloned.1.call-start = ((), (), s32[]{:S(2)}) async-start(), calls=%async_computation.10 | async-start | bytes 4325376 | tf_op jit(solution)/shard_map/reduce_scatter | solution.py:255
  447.1 81.6 %copy-start.4 = (f32[1024,512]{1,0:T(8,128)S(1)}, f32[1024,512]{1,0:T(8,128)}, u32[]{:S(2)}) copy-start(f32[1024,512]{1,0:T(8,128)} %copy-done.3) | copy-start | bytes 6291460
  522.8 228.4 %copy-start.1 = (bf16[256,512]{1,0:T(8,128)(2,1)S(1)}, bf16[256,512]{1,0:T(8,128)(2,1)}, u32[]{:S(2)}) copy-start(bf16[256,512]{1,0:T(8,128)(2,1)} %param.27) | copy-start | bytes 786436
  (37 other events, 107.8 us)
Sparse Core Ops, SparseCore 0:
  10.4 35.8 all-gather.4
  96.0 55.0 reduce-scatter.4
  275.3 31.9 all-gather.10
  432.1 32.4 reduce-scatter.6
  467.3 142.3 reduce-scatter.10
  612.4 138.6 reduce-scatter.8
Sparse Core Ops, SparseCore 1:
  99.9 78.4 all-gather.6
  181.7 55.4 all-gather.8
  427.2 93.5 all-reduce.3
where the time goes:
time: 767 us; the launch traced here: 759 us
  waiting for transfers between devices  434 us (57%)
  matrix products  185 us (24%)
  other arithmetic  42.2 us (6%)
  blocking collectives  40.4 us (5%)
  local copies, waits for them, and re-layouts  33.8 us (4%)
  between operations  16.6 us (2%)
    reduce_scatter x1, waiting for transfers between devices, body(): lax.psum_scatter(up_part, ('dp', 'head'), scatter_dimension=0, tiled=True)  141 us
    reduce_scatter x1, waiting for transfers between devices, body(): lax.psum_scatter(down_part, ('dp', 'head'), scatter_dimension=0, tiled=True)  78.2 us
    reduce_scatter x1, waiting for transfers between devices, body(): lax.psum_scatter(jnp.dot(window, output_weight, preferred_element_type=jn...  53.9 us
    psum x1, blocking collectives, body(): lax.psum((first_gain_part, first_shift_part, second_gain_part, second_shi...  40.4 us
    all_gather x1, waiting for transfers between devices, body(): lax.all_gather(down_weight, ('dp', 'head'), axis=0, tiled=True)  35 us
    all_gather x1, waiting for transfers between devices, body(): gathered = lax.all_gather(stream_x, 'head', axis=0, tiled=True)  34.5 us
    psum x1, waiting for transfers between devices, body(): lax.psum(proj_part.astype(jnp.bfloat16), 'dp').astype(jnp.float32)  32.5 us
    all_gather x1, waiting for transfers between devices, body(): portion = lax.all_gather(grad_branch, 'head', axis=0, tiled=True)  32.1 us
  transfers between devices with their start and end apart: 9, of which 8 were waited for; matrix products, arithmetic and copies ran while one was open for 8% of the time, Pallas kernels for 0%

commit v1 on v0

v1 whole, which is shorter than its diff:
```python
import math
import functools
import jax
import jax.numpy as jnp
from jax import lax
from jax.experimental import pallas as pl
from jax.experimental.pallas import tpu as pltpu
from jax.sharding import PartitionSpec as P

HEADS = 8

BF = jnp.bfloat16
F32 = jnp.float32
LOG2E = 1.4426950408889634
NEG = -1e30
BLK = 256
MIB = 1 << 20

def nn(a, b):
    return lax.dot_general(a, b, (((1,), (0,)), ((), ())), preferred_element_type=F32)
def nt(a, b):
    return lax.dot_general(a, b, (((1,), (1,)), ((), ())), preferred_element_type=F32)
def tn(a, b):
    return lax.dot_general(a, b, (((0,), (0,)), ((), ())), preferred_element_type=F32)

def fill_mask(seg_ref, keep_ref, mask_ref):
    seq = mask_ref.shape[0]
    seg = seg_ref[...]
    code = jnp.where(keep_ref[...] == 1, seg, -1)
    code_col = jnp.broadcast_to(code.astype(F32), (128, seq)).T
    seg_row = seg.astype(F32)
    for kb in range(seq // BLK):
        rows = slice(kb * BLK, (kb + 1) * BLK)
        width = seq - kb * BLK
        same = jnp.concatenate([code_col[rows]] * (width // 128), axis=1) == seg_row[:, kb * BLK:]
        key = lax.broadcasted_iota(jnp.int32, (BLK, width), 0)
        query = lax.broadcasted_iota(jnp.int32, (BLK, width), 1)
        ok = (same & (key <= query)) | (key == query)
        mask_ref[rows, kb * BLK:] = jnp.where(ok, 0.0, NEG)

def lane_half(arr, h):
    lane = lax.broadcasted_iota(jnp.int32, arr.shape, 1)
    return jnp.where((lane < 64) if h == 0 else (lane >= 64), arr, jnp.zeros_like(arr))

def attn_fwd_kernel(scale, x_ref, wq_ref, wk_ref, wv_ref, seg_ref, keep_ref,
                    q_ref, k_ref, v_ref, att_ref, lse_ref, mask_ref):
    seq = x_ref.shape[0]
    @pl.when(pl.program_id(0) == 0)
    def _():
        fill_mask(seg_ref, keep_ref, mask_ref)
    x = x_ref[...]
    q_ref[...] = nn(x, wq_ref[...]).astype(BF)
    k_ref[...] = nn(x, wk_ref[...]).astype(BF)
    v = nn(x, wv_ref[...]).astype(BF)
    v_ref[...] = v
    v_t = v.T
    for qb in range(seq // BLK):
        cols = slice(qb * BLK, (qb + 1) * BLK)
        length = (qb + 1) * BLK
        outs = []
        for h in range(2):
            qm = lane_half(q_ref[cols, :], h)
            s = nt(k_ref[:length, :], qm) * (scale * LOG2E) + mask_ref[:length, cols]
            m = jnp.max(s, axis=0, keepdims=True)
            p = jnp.exp2(s - m)
            l = jnp.sum(p, axis=0, keepdims=True)
            o = nn(v_t[64 * h:64 * h + 64, :length], p.astype(BF))
            outs.append(o / l)
            lse_ref[0, h:h + 1, cols] = m + jnp.log2(l)
        att_ref[cols, :] = jnp.concatenate(outs, axis=0).T.astype(BF)

def proj_spec(width, which):
    return pl.BlockSpec((None, width, 128), lambda p: (which, 0, p))

def attn_fwd(x, proj, seg, keep, scale):
    seq, width = x.shape
    pairs = proj.shape[2] // 128
    ospec = pl.BlockSpec((seq, 128), lambda p: (0, p))
    full = lambda shape: pl.BlockSpec(shape, lambda p: (0,) * len(shape))
    o = jax.ShapeDtypeStruct((seq, 128 * pairs), BF)
    return pl.pallas_call(
        functools.partial(attn_fwd_kernel, scale),
        grid=(pairs,),
        in_specs=[full((seq, width)), proj_spec(width, 0), proj_spec(width, 1), proj_spec(width, 2), full((1, seq)), full((1, seq))],
        out_specs=[ospec, ospec, ospec, ospec, pl.BlockSpec((1, 2, seq), lambda p: (p, 0, 0))],
        out_shape=[o, o, o, o, jax.ShapeDtypeStruct((pairs, 2, seq), F32)],
        scratch_shapes=[pltpu.VMEM((seq, seq), F32)],
        compiler_params=pltpu.CompilerParams(vmem_limit_bytes=56 * MIB),
        cost_estimate=pl.CostEstimate(flops=10**10, bytes_accessed=10**7, transcendentals=0),
        name="attn_fwd",
    )(x, proj, proj, proj, seg, keep)

def attn_bwd_kernel(scale, pairs, x_ref, wq_ref, wk_ref, wv_ref, q_ref, k_ref, v_ref, att_ref, do_ref, lse_ref, seg_ref, keep_ref, gm_ref,
                    sg_ref, dw_ref, mask_ref, xt_ref, dqt_ref, dkv_ref, acc_ref):
    seq = x_ref.shape[0]
    step = pl.program_id(0)
    @pl.when(step == 0)
    def _():
        fill_mask(seg_ref, keep_ref, mask_ref)
        xt_ref[...] = x_ref[...].T
        acc_ref[...] = gm_ref[...]
    prod = (do_ref[...].astype(F32) * att_ref[...].astype(F32)).T
    k_t = k_ref[...].T
    nb = seq // BLK
    for h in range(2):
        delta = jnp.sum(prod[64 * h:64 * h + 64], axis=0, keepdims=True)
        lse = lse_ref[0, h:h + 1, :]
        for kb in range(nb):
            rows = slice(kb * BLK, (kb + 1) * BLK)
            lo = kb * BLK
            qm = lane_half(q_ref[lo:, :], h)
            dom = lane_half(do_ref[lo:, :], h)
            s = nt(k_ref[rows, :], qm) * (scale * LOG2E) + mask_ref[rows, lo:]
            p = jnp.exp2(s - lse[:, lo:])
            dp = nt(v_ref[rows, :], dom)
            ds = (p * (dp - delta[:, lo:])).astype(BF)
            dv = nn(p.astype(BF), dom)
            dk = nn(ds, qm) * scale
            dq = nn(k_t[64 * h:64 * h + 64, rows], ds)
            if h == 0:
                dkv_ref[rows, 0:128] = dk
                dkv_ref[rows, 128:256] = dv
            else:
                dkv_ref[rows, 0:128] += dk
                dkv_ref[rows, 128:256] += dv
            if kb == 0:
                dqt_ref[64 * h:64 * h + 64, :] = dq
            else:
                dqt_ref[64 * h:64 * h + 64, lo:] += dq
    dq = (dqt_ref[...] * scale).T.astype(BF)
    g = jnp.concatenate([dq, dkv_ref[...].astype(BF)], axis=1)
    dw_ref[0] = nn(xt_ref[...], g).astype(BF)
    w = jnp.concatenate([wq_ref[...], wk_ref[...], wv_ref[...]], axis=1)
    acc_ref[...] += nt(g, w)
    @pl.when(step == pairs - 1)
    def _():
        sg_ref[...] = acc_ref[...]

def attn_bwd(x, proj, q, k, v, att, do, lse, seg, keep, gm, scale):
    seq, width = x.shape
    pairs = proj.shape[2] // 128
    ospec = pl.BlockSpec((seq, 128), lambda p: (0, p))
    full = lambda shape: pl.BlockSpec(shape, lambda p: (0,) * len(shape))
    return pl.pallas_call(
        functools.partial(attn_bwd_kernel, scale, pairs),
        grid=(pairs,),
        in_specs=[full((seq, width)), proj_spec(width, 0), proj_spec(width, 1), proj_spec(width, 2), ospec, ospec, ospec, ospec, ospec, pl.BlockSpec((1, 2, seq), lambda p: (p, 0, 0)), full((1, seq)), full((1, seq)), full((seq, width))],
        out_specs=[full((seq, width)), pl.BlockSpec((1, width, 384), lambda p: (p, 0, 0))],
        out_shape=[jax.ShapeDtypeStruct((seq, width), F32), jax.ShapeDtypeStruct((pairs, width, 384), BF)],
        scratch_shapes=[pltpu.VMEM((seq, seq), F32), pltpu.VMEM((width, seq), BF), pltpu.VMEM((128, seq), F32), pltpu.VMEM((seq, 256), F32), pltpu.VMEM((seq, width), F32)],
        compiler_params=pltpu.CompilerParams(vmem_limit_bytes=56 * MIB),
        cost_estimate=pl.CostEstimate(flops=10**10, bytes_accessed=10**7, transcendentals=0),
        name="attn_bwd",
    )(x, proj, proj, proj, q, k, v, att, do, lse, seg, keep, gm)

def gelu_parts(h):
    e = jnp.exp2(h * h * (-0.5 * LOG2E))
    t = pl.reciprocal(1.0 + (0.3275911 / math.sqrt(2.0)) * jnp.abs(h), approx=False)
    poly = ((((0.5 * 1.061405429) * t - 0.5 * 1.453152027) * t + 0.5 * 1.421413741) * t - 0.5 * 0.284496736) * t + 0.5 * 0.254829592
    tail = poly * t * e
    phi = jnp.where(h >= 0, 1.0 - tail, tail)
    return h * phi, phi + h * e * (1.0 / math.sqrt(2.0 * math.pi))

def mean_of(v):
    return jnp.sum(v, axis=-1, keepdims=True) * (1.0 / v.shape[-1])

def dense_kernel(x_ref, y_ref, att_ref, gs_ref, gd_ref, wo_ref, up_ref, down_ref, g1_ref, b1_ref, g2_ref, b2_ref,
                 ns_ref, nd_ref, act_ref, dh_ref, gf_ref, fl_ref, gm_ref, gb_ref, do_ref, vec_ref, der_ref):
    @pl.when(pl.program_id(0) == 0)
    def _():
        vec_ref[...] = jnp.zeros_like(vec_ref)
    branch = nn(att_ref[...], wo_ref[...])
    mixed = x_ref[...].astype(F32) + branch
    c1 = mixed - mean_of(mixed)
    rstd1 = lax.rsqrt(mean_of(c1 * c1) + 1e-5)
    zhat1 = c1 * rstd1
    first = zhat1 * g1_ref[...] + b1_ref[...]
    low = first.astype(BF)
    fl_ref[...] = low
    ff = up_ref.shape[0]
    CH = 512
    for c in range(ff // CH):
        cs = slice(c * CH, (c + 1) * CH)
        val, der = gelu_parts(nt(low, up_ref[cs, :]))
        act_ref[:, cs] = val.astype(BF)
        der_ref[:, cs] = der
    ffn = nn(act_ref[...], down_ref[...])
    z2 = first + ffn
    c2 = z2 - mean_of(z2)
    rstd2 = lax.rsqrt(mean_of(c2 * c2) + 1e-5)
    zhat2 = c2 * rstd2
    ns_ref[...] = (zhat2 * g2_ref[...] + b2_ref[...]).astype(BF)
    nd_ref[...] = (y_ref[...].astype(F32) + branch + ffn).astype(BF)
    u = gs_ref[...].astype(F32)
    w = u * g2_ref[...]
    second = rstd2 * (w - mean_of(w) - zhat2 * mean_of(w * zhat2))
    gd = gd_ref[...].astype(F32)
    gf = (second + gd).astype(BF)
    gf_ref[...] = gf
    for c in range(ff // CH):
        cs = slice(c * CH, (c + 1) * CH)
        dh_ref[:, cs] = (nt(gf, down_ref[cs, :]) * der_ref[:, cs]).astype(BF)
    gfirst = second + nn(dh_ref[...], up_ref[...])
    w1 = gfirst * g1_ref[...]
    gm = rstd1 * (w1 - mean_of(w1) - zhat1 * mean_of(w1 * zhat1))
    gm_ref[...] = gm
    gb = (gm + gd).astype(BF)
    gb_ref[...] = gb
    do_ref[...] = nt(gb, wo_ref[...]).astype(BF)
    fold = lambda v: jnp.sum(v, axis=0, keepdims=True)
    vec_ref[...] += jnp.concatenate([fold(gfirst * zhat1), fold(gfirst), fold(u * zhat2), fold(u), jnp.zeros((4, u.shape[1]), F32)], axis=0)

def dense(x, y, att, gs, gd, wo, ffw, g1, b1, g2, b2, blk=256):
    seq, width = x.shape
    ff = ffw.shape[1]
    ffspec = lambda which: pl.BlockSpec((None, ff, width), lambda p: (which, 0, 0))
    row = lambda w: pl.BlockSpec((blk, w), lambda p: (p, 0))
    full = lambda shape: pl.BlockSpec(shape, lambda p: (0,) * len(shape))
    sd = lambda w, t: jax.ShapeDtypeStruct((seq, w), t)
    return pl.pallas_call(
        dense_kernel,
        grid=(seq // blk,),
        in_specs=[row(width)] * 5 + [full(wo.shape), ffspec(0), ffspec(1)] + [full((1, width))] * 4,
        out_specs=[row(width), row(width), row(ff), row(ff), row(width), row(width), row(width), row(width), row(width), full((8, width))],
        out_shape=[sd(width, BF), sd(width, BF), sd(ff, BF), sd(ff, BF), sd(width, BF), sd(width, BF), sd(width, F32), sd(width, BF), sd(width, BF), jax.ShapeDtypeStruct((8, width), F32)],
        scratch_shapes=[pltpu.VMEM((blk, ff), F32)],
        compiler_params=pltpu.CompilerParams(vmem_limit_bytes=56 * MIB),
        cost_estimate=pl.CostEstimate(flops=2 * 10**10, bytes_accessed=2 * 10**7, transcendentals=0),
        name="dense",
    )(x, y, att, gs, gd, wo, ffw, ffw, g1, b1, g2, b2)

def wgrad_kernel(a_ref, g_ref, dh_ref, fl_ref, out_ref):
    out_ref[0] = tn(dh_ref[...], fl_ref[...]).astype(BF)
    out_ref[1] = tn(a_ref[...], g_ref[...]).astype(BF)

def wgrad(act, gf, dh, fl, part, steps=2):
    seq, ff = act.shape
    width = gf.shape[1]
    b = ff // 2 // steps
    full = lambda shape: pl.BlockSpec(shape, lambda p: (0,) * len(shape))
    cols = pl.BlockSpec((seq, b), lambda p: (0, p + part * steps))
    return pl.pallas_call(
        wgrad_kernel,
        grid=(steps,),
        in_specs=[cols, full((seq, width)), cols, full((seq, width))],
        out_specs=pl.BlockSpec((2, b, width), lambda p: (0, p, 0)),
        out_shape=jax.ShapeDtypeStruct((2, ff // 2, width), BF),
        compiler_params=pltpu.CompilerParams(vmem_limit_bytes=56 * MIB),
        cost_estimate=pl.CostEstimate(flops=5 * 10**9, bytes_accessed=10**7, transcendentals=0),
        name="wgrad",
    )(act, gf, dh, fl)

def ograd_kernel(a_ref, g_ref, out_ref):
    out_ref[...] = tn(a_ref[...], g_ref[...]).astype(BF)

def ograd(att, gb):
    return pl.pallas_call(
        ograd_kernel,
        out_shape=jax.ShapeDtypeStruct((att.shape[1], gb.shape[1]), BF),
        compiler_params=pltpu.CompilerParams(vmem_limit_bytes=56 * MIB),
        cost_estimate=pl.CostEstimate(flops=10**9, bytes_accessed=2 * 10**6, transcendentals=0),
        name="ograd",
    )(att, gb)


def body(
    dp_size,
    head_size,
    stream_x,
    stream_y,
    segments,
    keep_mask,
    query_weight,
    key_weight,
    value_weight,
    output_weight,
    first_gain,
    first_shift,
    up_weight,
    down_weight,
    second_gain,
    second_shift,
    grad_stream,
    grad_dual,
):
    seq, width = stream_x.shape
    cols = query_weight.shape[1]
    scale = 1.0 / math.sqrt(width // HEADS)
    axes = ("dp", "head")
    total = dp_size * head_size
    core_step = head_size
    head_steps = [1 << b for b in range(head_size.bit_length() - 1)]
    chip_steps = [core_step << b for b in range(1, dp_size.bit_length() - 1)]

    def swap(value, even_step, odd_step=None):
        odd_step = even_step if odd_step is None else odd_step
        pairs = [
            (i, i ^ (odd_step if i // core_step % 2 else even_step)) for i in range(total)
        ]
        return lax.ppermute(value, axes, pairs)

    head_index = lax.axis_index("head")
    core = lax.axis_index("dp") % 2
    seg = lax.dynamic_slice_in_dim(segments, head_index * seq, seq).reshape(1, seq)
    keep = lax.dynamic_slice_in_dim(keep_mask, head_index * seq, seq).reshape(1, seq)

    proj = jnp.stack([query_weight, key_weight, value_weight])
    outw = output_weight
    for step in head_steps:
        proj = jnp.concatenate([proj, swap(proj, step)], axis=2)
        outw = jnp.concatenate([outw, swap(outw, step)], axis=0)

    even = [chip_steps[-1]] + chip_steps[:-1] + head_steps
    odd = [chip_steps[-1]] + chip_steps[1:-1] + head_steps + chip_steps[:1]
    ffw = jnp.stack([up_weight, down_weight])
    for a, b in zip(even, odd):
        ffw = jnp.concatenate([ffw, swap(ffw, a, b)], axis=1)
    ffw = jnp.concatenate([ffw, swap(ffw, core_step)], axis=1)

    q, k, v, att, lse = attn_fwd(stream_x, proj, seg, keep, scale)
    row = lambda vec: vec.reshape(1, width)
    ns, nd, act, dh, gf, low, gm, gb, do, vec = dense(
        stream_x, stream_y, att, grad_stream, grad_dual, outw, ffw,
        row(first_gain), row(first_shift), row(second_gain), row(second_shift),
    )
    half = ffw.shape[1] // 2
    upper = wgrad(act, gf, dh, low, 1)
    sent = swap(upper, core_step)
    lower = wgrad(act, gf, dh, low, 0)
    out_part = ograd(att, gb)
    part = lower + sent
    for a, b in zip(even[::-1], odd[::-1]):
        half = part.shape[1] // 2
        recv = swap(part[:, half:], a, b)
        if half == up_weight.shape[0]:
            part = part[:, :half].astype(F32) + recv.astype(F32)
        else:
            part = part[:, :half] + recv
    up_grad, down_grad = part[0], part[1]

    sg, dw = attn_bwd(stream_x, proj, q, k, v, att, do, lse, seg, keep, gm, scale)

    pairs = dw.shape[0]
    dw = dw.reshape(pairs, width, 3, 128).transpose(2, 1, 0, 3).reshape(3, width, width)
    for step in head_steps[::-1]:
        n = dw.shape[2] // 2
        dw = dw[:, :, :n] + swap(dw[:, :, n:], step)
        out_part = out_part[:n] + swap(out_part[n:], step)
        vec = vec + swap(vec, step)
    for step in [core_step] + chip_steps:
        dw = dw + swap(dw, step)
        out_part = out_part + swap(out_part, step)
        vec = vec + swap(vec, step)
    dw = dw.astype(F32)
    return (
        ns, nd, sg, dw[0], dw[1], dw[2], out_part.astype(F32),
        vec[0], vec[1], up_grad, down_grad, vec[2], vec[3],
    )


def solution(mesh):
    both = ("dp", "head")
    rows, cols, whole = P(both, None), P(None, "head"), P()
    in_specs = (
        rows, rows, P("dp"), P("dp"), cols, cols, cols, P("head", None),
        whole, whole, rows, rows, whole, whole, rows, rows,
    )
    out_specs = (
        rows, rows, rows, cols, cols, cols, P("head", None),
        whole, whole, rows, rows, whole, whole,
    )
    inner = functools.partial(body, mesh.shape["dp"], mesh.shape["head"])
    return jax.shard_map(inner, mesh=mesh, in_specs=in_specs, out_specs=out_specs, check_vma=False)
```

time: 767 us -> 301 us (0.39)
  waiting for transfers between devices: 434 us -> 149 us
  matrix products: 185 us -> 0 us
  Pallas kernels: 0 us -> 84.9 us
  blocking collectives: 40.4 us -> 0 us
  starting transfers between devices: 0.37 us -> 36 us
  other arithmetic: 42.2 us -> 13.7 us
  local copies, waits for them, and re-layouts: 33.8 us -> 15.3 us
  between operations: 16.6 us -> 0.92 us
    reduce_scatter x4 -> x0, waiting for transfers between devices: 274 us -> none  [the longest x1 141 us: body(): lax.psum_scatter(up_part, ('dp', 'head'), scatter_dimension=0, tiled=True)]
    dot_general x40 -> x0, matrix products: 185 us -> none  [the longest x8 28.7 us: masked_scores(): jnp.einsum('hqd,hkd->hqk', query_block, key_rows, preferred_element_type=...]
    ppermute x0 -> x27, waiting for transfers between devices: none -> 149 us  [swap(): return lax.ppermute(value, axes, pairs)]
    all_gather x4 -> x0, waiting for transfers between devices: 126 us -> none  [the longest x1 35 us: body(): lax.all_gather(down_weight, ('dp', 'head'), axis=0, tiled=True)]
    pallas_call x0 -> x6, Pallas kernels: none -> 84.9 us  [the longest x1 24.7 us: attn_bwd(): pl.pallas_call(functools.partial(attn_bwd_kernel, scale, pairs), grid=(pa...]
    psum x1 -> x0, blocking collectives: 40.4 us -> none  [body(): lax.psum((first_gain_part, first_shift_part, second_gain_part, second_shi...]
    ppermute x0 -> x27, starting transfers between devices: none -> 36 us  [swap(): return lax.ppermute(value, axes, pairs)]
    psum x1 -> x0, waiting for transfers between devices: 32.5 us -> none  [body(): lax.psum(proj_part.astype(jnp.bfloat16), 'dp').astype(jnp.float32)]
  transfers between devices with their start and end apart: 9 -> 27, of which waited for: 8 -> 16; matrix products, arithmetic and copies ran while one was open for 8% -> 7% of each run, Pallas kernels for 0% -> 18%
where the time goes in v1:
time: 301 us; the launch traced here: 300 us
  waiting for transfers between devices  149 us (50%)
  Pallas kernels  84.9 us (28%)
  starting transfers between devices  36 us (12%)
  local copies, waits for them, and re-layouts  15.3 us (5%)
  other arithmetic  13.7 us (5%)
    ppermute x27, waiting for transfers between devices, swap(): return lax.ppermute(value, axes, pairs)  149 us
    ppermute x27, starting transfers between devices, swap(): return lax.ppermute(value, axes, pairs)  36 us
    pallas_call x1, Pallas kernels, attn_bwd(): pl.pallas_call(functools.partial(attn_bwd_kernel, scale, pairs), grid=(pa...  24.7 us
    pallas_call x1, Pallas kernels, dense(): pl.pallas_call(dense_kernel, grid=(seq // blk,), in_specs=[row(width)] *...  24.1 us
    pallas_call x1, Pallas kernels, attn_fwd(): pl.pallas_call(functools.partial(attn_fwd_kernel, scale), grid=(pairs,),...  21.5 us
    pallas_call x2, Pallas kernels, wgrad(): pl.pallas_call(wgrad_kernel, grid=(steps,), in_specs=[cols, full((seq, wi...  11.6 us
    unnamed x30, local copies, waits for them, and re-layouts  8.45 us
  transfers between devices with their start and end apart: 27, of which 16 were waited for; matrix products, arithmetic and copies ran while one was open for 7% of the time, Pallas kernels for 18%

profile of v1, /device:TPU:0, one launch (start us, length us, event | category | flops | bytes accessed | tf_op | source)
XLA Modules:
  0.0 299.9 jit_solution(6407125206371677560)
XLA Ops:
  2.3 4.0 %collective-permute-start.2 = (bf16[2,64,512]{2,1,0:T(8,128)(2,1)S(1)}, bf16[2,64,512]{2,1,0:T(8,128)(2,1)S(1)}, u32[]{:S(2)}, u32[]{:S(2)}) collective-permute-start(bf16[2,64,512]{2,1,0:T(8,128)(2,1)S(1)} %get-tuple-element.75), channel_id=1, source_target_pairs={{0,16},{1,17},{2,18},{3,19},{4,20},{5,21},{6,22},{7,23},{8,24},{9,... | collective-permute-start | bytes 393224 | tf_op jit(solution)/shard_map/ppermute | solution.py:300
  6.3 6.3 %collective-permute-done.2 = bf16[2,64,512]{2,1,0:T(8,128)(2,1)S(1)} collective-permute-done((bf16[2,64,512]{2,1,0:T(8,128)(2,1)S(1)}, bf16[2,64,512]{2,1,0:T(8,128)(2,1)S(1)}, u32[]{:S(2)}, u32[]{:S(2)}) %collective-permute-start.2) | collective-permute-done | bytes 131104 | tf_op jit(solution)/shard_map/ppermute | solution.py:300
  15.1 4.8 %collective-permute-done.3 = bf16[2,128,512]{2,1,0:T(8,128)(2,1)S(1)} collective-permute-done((bf16[2,128,512]{2,1,0:T(8,128)(2,1)S(1)}, bf16[2,128,512]{2,1,0:T(8,128)(2,1)S(1)}, u32[]{:S(2)}, u32[]{:S(2)}) %collective-permute-start.3) | collective-permute-done | bytes 262176 | tf_op jit(solution)/shard_map/ppermute | solution.py:300
  21.6 8.5 %collective-permute-done.4 = bf16[2,256,512]{2,1,0:T(8,128)(2,1)S(1)} collective-permute-done((bf16[2,256,512]{2,1,0:T(8,128)(2,1)S(1)}, bf16[2,256,512]{2,1,0:T(8,128)(2,1)S(1)}, u32[]{:S(2)}, u32[]{:S(2)}) %collective-permute-start.4) | collective-permute-done | bytes 524320 | tf_op jit(solution)/shard_map/ppermute | solution.py:300
  34.0 11.0 %collective-permute-done.5 = bf16[2,512,512]{2,1,0:T(8,128)(2,1)S(1)} collective-permute-done((bf16[2,512,512]{2,1,0:T(8,128)(2,1)S(1)}, bf16[2,512,512]{2,1,0:T(8,128)(2,1)S(1)}, u32[]{:S(2)}, u32[]{:S(2)}) %collective-permute-start.5) | collective-permute-done | bytes 1048608 | tf_op jit(solution)/shard_map/ppermute | solution.py:300
  51.6 21.3 %collective-permute-done.1 = bf16[256,512]{1,0:T(8,128)(2,1)S(1)} collective-permute-done((bf16[256,512]{1,0:T(8,128)(2,1)S(1)}, bf16[256,512]{1,0:T(8,128)(2,1)S(1)}, u32[]{:S(2)}, u32[]{:S(2)}) %collective-permute-start.1) | collective-permute-done | bytes 262176 | tf_op jit(solution)/shard_map/ppermute | solution.py:300
  73.7 2.4 pad_maximum_fusion.wq_ref.wk_ref.wv_ref
  76.1 21.5 %attn_fwd.1 = (bf16[1024,512]{1,0:T(8,128)(2,1)}, bf16[1024,512]{1,0:T(8,128)(2,1)}, bf16[1024,512]{1,0:T(8,128)(2,1)}, bf16[1024,512]{1,0:T(8,128)(2,1)}, f32[4,2,1024]{2,1,0:T(2,128)}) custom-call(bf16[1024,512]{1,0:T(8,128)(2,1)} %x_ref.5, bf16[3,512,512]{2,1,0:T(8,128)(2,1)} %pad_maximum_fusion.wq_ref.wk_ref.wv_ref, ...), custom_call_target="tpu_custom_call" | custom-call | flops 10000000000 | bytes 10000000 | tf_op jit(solution)/shard_map/attn_fwd/pallas_call | solution.py:81
  99.8 24.1 %dense.1 = (bf16[1024,512]{1,0:T(8,128)(2,1)}, bf16[1024,512]{1,0:T(8,128)(2,1)}, bf16[1024,2048]{1,0:T(8,128)(2,1)}, bf16[1024,2048]{1,0:T(8,128)(2,1)}, bf16[1...) custom-call(bf16[1024,512]{1,0:T(8,128)(2,1)} %x_ref.5, ...), custom_call_target="tpu_custom_call" | custom-call | flops 20000000000 | bytes 20000000 | tf_op jit(solution)/shard_map/dense/pallas_call | solution.py:220
  123.9 5.8 %wgrad.3 = bf16[2,1024,512]{2,1,0:T(8,128)(2,1)} custom-call(bf16[1024,2048]{1,0:T(8,128)(2,1)} %get-tuple-element.43.a_ref, bf16[1024,512]{1,0:T(8,128)(2,1)} %get-tuple-element.44.g_ref, bf16[1024,2048]{1,0:T(8,128)(2,1)} %get-tuple-element.45.dh_ref, bf16[1024,512]{1,0:T(8,128)(2,1)} %get-tuple-element.46.fl_ref), custom_call_target="tpu_custom_call" | custom-call | flops 5000000000 | bytes 10000000 | tf_op jit(solution)/shard_map/wgrad/pallas_call | solution.py:242
  129.7 24.7 %attn_bwd.1 = (f32[1024,512]{1,0:T(8,128)}, bf16[4,512,384]{2,1,0:T(8,128)(2,1)}) custom-call(bf16[1024,512]{1,0:T(8,128)(2,1)} %x_ref.5, bf16[3,512,512]{2,1,0:T(8,128)(2,1)} %pad_maximum_fusion.wq_ref.wk_ref.wv_ref, bf16[3,512,512]{2,1,0:T(8,128)(2,1)} %pad_maximum_fusion.wq_ref.wk_ref.wv_ref, bf16[3,512,512]{2,1,0:T(8,128)(2,1)} %pad_maximum_fusion.wq_ref.wk_ref.wv_ref, ...), custom_call_target="tpu_custom_call" | custom-call | flops 10000000000 | bytes 10000000 | tf_op jit(solution)/shard_map/attn_bwd/pallas_call | solution.py:144
  157.9 18.4 %collective-permute-done.7 = bf16[3,512,256]{1,2,0:T(8,128)(2,1)S(1)} collective-permute-done((bf16[3,512,256]{1,2,0:T(8,128)(2,1)S(1)}, bf16[3,512,256]{1,2,0:T(8,128)(2,1)S(1)}, u32[]{:S(2)}, u32[]{:S(2)}) %collective-permute-start.7) | collective-permute-done | bytes 786464 | tf_op jit(solution)/shard_map/ppermute | solution.py:300
  176.5 5.8 %wgrad.2 = bf16[2,1024,512]{2,1,0:T(8,128)(2,1)} custom-call(bf16[1024,2048]{1,0:T(8,128)(2,1)} %get-tuple-element.43.a_ref, bf16[1024,512]{1,0:T(8,128)(2,1)} %get-tuple-element.44.g_ref, bf16[1024,2048]{1,0:T(8,128)(2,1)} %get-tuple-element.45.dh_ref, bf16[1024,512]{1,0:T(8,128)(2,1)} %get-tuple-element.46.fl_ref), custom_call_target="tpu_custom_call" | custom-call | flops 5000000000 | bytes 10000000 | tf_op jit(solution)/shard_map/wgrad/pallas_call | solution.py:242
  182.3 2.8 add.80
  188.6 3.1 %ograd.1 = bf16[512,512]{1,0:T(8,128)(2,1)} custom-call(bf16[1024,512]{1,0:T(8,128)(2,1)} %get-tuple-element.30.att_ref.a_ref, bf16[1024,512]{1,0:T(8,128)(2,1)} %get-tuple-element.41.g_ref), custom_call_target="tpu_custom_call" | custom-call | flops 1000000000 | bytes 2000000 | tf_op jit(solution)/shard_map/ograd/pallas_call | solution.py:257
  193.2 12.4 %collective-permute-done.12 = bf16[256,512]{1,0:T(8,128)(2,1)S(1)} collective-permute-done((bf16[256,512]{1,0:T(8,128)(2,1)S(1)}, bf16[256,512]{1,0:T(8,128)(2,1)S(1)}, u32[]{:S(2)}, u32[]{:S(2)}) %collective-permute-start.12) | collective-permute-done | bytes 262176 | tf_op jit(solution)/shard_map/ppermute | solution.py:300
  212.5 5.1 %collective-permute-done.14 = bf16[256,512]{1,0:T(8,128)(2,1)S(1)} collective-permute-done((bf16[256,512]{1,0:T(8,128)(2,1)S(1)}, bf16[256,512]{1,0:T(8,128)(2,1)S(1)}, u32[]{:S(2)}, u32[]{:S(2)}) %collective-permute-start.14) | collective-permute-done | bytes 262176 | tf_op jit(solution)/shard_map/ppermute | solution.py:300
  220.0 2.2 collective-permute-done.17
  222.2 6.6 %collective-permute-start.18 = (f32[8,512]{1,0:T(8,128)S(1)}, f32[8,512]{1,0:T(8,128)S(1)}, u32[]{:S(2)}, u32[]{:S(2)}) collective-permute-start(f32[8,512]{1,0:T(8,128)S(1)} %add.75), channel_id=1, source_target_pairs={{0,2},{1,3},{2,0},{3,1},{4,6},{5,7},{6,4},{7,5},{8,10},{9,11},{10,... | collective-permute-start | bytes 49160 | tf_op jit(solution)/shard_map/ppermute | solution.py:300
  231.1 2.3 collective-permute-done.19
  234.7 4.7 %collective-permute-done.20 = f32[8,512]{1,0:T(8,128)S(1)} collective-permute-done((f32[8,512]{1,0:T(8,128)S(1)}, f32[8,512]{1,0:T(8,128)S(1)}, u32[]{:S(2)}, u32[]{:S(2)}) %collective-permute-start.20) | collective-permute-done | bytes 16416 | tf_op jit(solution)/shard_map/ppermute | solution.py:300
  241.1 2.9 collective-permute-done.21
  248.2 28.0 %collective-permute-done.16 = bf16[256,512]{1,0:T(8,128)(2,1)S(1)} collective-permute-done((bf16[256,512]{1,0:T(8,128)(2,1)S(1)}, bf16[256,512]{1,0:T(8,128)(2,1)S(1)}, u32[]{:S(2)}, u32[]{:S(2)}) %collective-permute-start.16) | collective-permute-done | bytes 262176 | tf_op jit(solution)/shard_map/ppermute | solution.py:300
  277.2 18.7 %collective-permute-done.11 = bf16[3,512,256]{1,2,0:T(8,128)(2,1)S(1)} collective-permute-done((bf16[3,512,256]{1,2,0:T(8,128)(2,1)S(1)}, bf16[3,512,256]{1,2,0:T(8,128)(2,1)S(1)}, u32[]{:S(2)}, u32[]{:S(2)}) %collective-permute-start.11) | collective-permute-done | bytes 786464 | tf_op jit(solution)/shard_map/ppermute | solution.py:300
  (108 shorter events, 51.5 us)
Async XLA Ops:
  2.3 10.3 %collective-permute-start.2 = (bf16[2,64,512]{2,1,0:T(8,128)(2,1)S(1)}, bf16[2,64,512]{2,1,0:T(8,128)(2,1)S(1)}, u32[]{:S(2)}, u32[]{:S(2)}) collective-permute-start(bf16[2,64,512]{2,1,0:T(8,128)(2,1)S(1)} %get-tuple-element.75), channel_id=1, source_target_pairs={{0,16},{1,17},{2,18},{3,19},{4,20},{5,21},{6,22},{7,23},{8,24},{9,... | collective-permute-start | bytes 393224 | tf_op jit(solution)/shard_map/ppermute | solution.py:300
  13.5 6.4 %collective-permute-start.3 = (bf16[2,128,512]{2,1,0:T(8,128)(2,1)S(1)}, bf16[2,128,512]{2,1,0:T(8,128)(2,1)S(1)}, u32[]{:S(2)}, u32[]{:S(2)}) collective-permute-start(bf16[2,128,512]{2,1,0:T(8,128)(2,1)S(1)} %pad_maximum_fusion.5), channel_id=1, source_target_pairs={{0,4},{1,5},{2,10},{3,11},{4,0},{5,1},{6,14},{7,15},{8,12},{9,13},... | collective-permute-start | bytes 786440 | tf_op jit(solution)/shard_map/ppermute | solution.py:300
  20.8 9.2 %collective-permute-start.4 = (bf16[2,256,512]{2,1,0:T(8,128)(2,1)S(1)}, bf16[2,256,512]{2,1,0:T(8,128)(2,1)S(1)}, u32[]{:S(2)}, u32[]{:S(2)}) collective-permute-start(bf16[2,256,512]{2,1,0:T(8,128)(2,1)S(1)} %pad_maximum_fusion.4), channel_id=1, source_target_pairs={{0,8},{1,9},{2,3},{3,2},{4,12},{5,13},{6,7},{7,6},{8,0},{9,1},{10,... | collective-permute-start | bytes 1572872 | tf_op jit(solution)/shard_map/ppermute | solution.py:300
  30.2 14.9 %collective-permute-start.5 = (bf16[2,512,512]{2,1,0:T(8,128)(2,1)S(1)}, bf16[2,512,512]{2,1,0:T(8,128)(2,1)S(1)}, u32[]{:S(2)}, u32[]{:S(2)}) collective-permute-start(bf16[2,512,512]{2,1,0:T(8,128)(2,1)S(1)} %pad_maximum_fusion.1), channel_id=1, source_target_pairs={{0,1},{1,0},{2,6},{3,7},{4,5},{5,4},{6,2},{7,3},{8,9},{9,8},{10,14... | collective-permute-start | bytes 3145736 | tf_op jit(solution)/shard_map/ppermute | solution.py:300
  46.1 51.5 %collective-permute-start.6 = (bf16[2,1024,512]{2,1,0:T(8,128)(2,1)}, bf16[2,1024,512]{2,1,0:T(8,128)(2,1)S(1)}, u32[]{:S(2)}, u32[]{:S(2)}) collective-permute-start(bf16[2,1024,512]{2,1,0:T(8,128)(2,1)} %get-tuple-element.63), channel_id=1, source_target_pairs={{0,2},{1,3},{2,0},{3,1},{4,6},{5,7},{6,4},{7,5},{8,10},{9,11},{10,... | collective-permute-start | bytes 6291464 | tf_op jit(solution)/shard_map/ppermute | solution.py:300
  48.4 25.4 %collective-permute-start = (bf16[3,512,256]{2,1,0:T(8,128)(2,1)}, bf16[3,512,256]{2,1,0:T(8,128)(2,1)}, u32[]{:S(2)}, u32[]{:S(2)}) collective-permute-start(bf16[3,512,256]{2,1,0:T(8,128)(2,1)} %pad_maximum_fusion.2), channel_id=1, source_target_pairs={{0,1},{1,0},{2,3},{3,2},{4,5},{5,4},{6,7},{7,6},{8,9},{9,8},{10,11... | collective-permute-start | bytes 2359304 | tf_op jit(solution)/shard_map/ppermute | solution.py:300
  49.9 23.0 %collective-permute-start.1 = (bf16[256,512]{1,0:T(8,128)(2,1)S(1)}, bf16[256,512]{1,0:T(8,128)(2,1)S(1)}, u32[]{:S(2)}, u32[]{:S(2)}) collective-permute-start(bf16[256,512]{1,0:T(8,128)(2,1)S(1)} %copy-done.5), channel_id=1, source_target_pairs={{0,1},{1,0},{2,3},{3,2},{4,5},{5,4},{6,7},{7,6},{8,9},{9,8},{10,11... | collective-permute-start | bytes 786440 | tf_op jit(solution)/shard_map/ppermute | solution.py:300
  129.7 52.6 %collective-permute-start.22 = (bf16[2,1024,512]{2,1,0:T(8,128)(2,1)}, bf16[2,1024,512]{2,1,0:T(8,128)(2,1)}, u32[]{:S(2)}, u32[]{:S(2)}) collective-permute-start(bf16[2,1024,512]{2,1,0:T(8,128)(2,1)} %wgrad.3), channel_id=1, source_target_pairs={{0,2},{1,3},{2,0},{3,1},{4,6},{5,7},{6,4},{7,5},{8,10},{9,11},{10,... | collective-permute-start | bytes 6291464 | tf_op jit(solution)/shard_map/ppermute | solution.py:300
  156.3 20.0 %collective-permute-start.7 = (bf16[3,512,256]{1,2,0:T(8,128)(2,1)S(1)}, bf16[3,512,256]{1,2,0:T(8,128)(2,1)S(1)}, u32[]{:S(2)}, u32[]{:S(2)}) collective-permute-start(bf16[3,512,256]{1,2,0:T(8,128)(2,1)S(1)} %slice.85), channel_id=1, source_target_pairs={{0,1},{1,0},{2,3},{3,2},{4,5},{5,4},{6,7},{7,6},{8,9},{9,8},{10,11... | collective-permute-start | bytes 2359304 | tf_op jit(solution)/shard_map/ppermute | solution.py:300
  176.4 10.4 %collective-permute-start.8 = (bf16[3,512,256]{1,2,0:T(8,128)(2,1)S(1)}, bf16[3,512,256]{1,2,0:T(8,128)(2,1)S(1)}, u32[]{:S(2)}, u32[]{:S(2)}) collective-permute-start(bf16[3,512,256]{1,2,0:T(8,128)(2,1)S(1)} %slice_add_fusion.1), channel_id=1, source_target_pairs={{0,2},{1,3},{2,0},{3,1},{4,6},{5,7},{6,4},{7,5},{8,10},{9,11},{10,... | collective-permute-start | bytes 2359304 | tf_op jit(solution)/shard_map/ppermute | solution.py:300
  185.2 25.7 %collective-permute-start.23 = (bf16[2,512,512]{2,1,0:T(8,128)(2,1)S(1)}, bf16[2,512,512]{2,1,0:T(8,128)(2,1)S(1)}, u32[]{:S(2)}, u32[]{:S(2)}) collective-permute-start(bf16[2,512,512]{2,1,0:T(8,128)(2,1)S(1)} %slice.94), channel_id=1, source_target_pairs={{0,1},{1,0},{2,6},{3,7},{4,5},{5,4},{6,2},{7,3},{8,9},{9,8},{10,14... | collective-permute-start | bytes 3145736 | tf_op jit(solution)/shard_map/ppermute | solution.py:300
  187.0 22.9 %collective-permute-start.9 = (bf16[3,512,256]{1,2,0:T(8,128)(2,1)S(1)}, bf16[3,512,256]{1,2,0:T(8,128)(2,1)S(1)}, u32[]{:S(2)}, u32[]{:S(2)}) collective-permute-start(bf16[3,512,256]{1,2,0:T(8,128)(2,1)S(1)} %add.66), channel_id=1, source_target_pairs={{0,4},{1,5},{2,6},{3,7},{4,0},{5,1},{6,2},{7,3},{8,12},{9,13},{10,... | collective-permute-start | bytes 2359304 | tf_op jit(solution)/shard_map/ppermute | solution.py:300
  192.7 13.0 %collective-permute-start.12 = (bf16[256,512]{1,0:T(8,128)(2,1)S(1)}, bf16[256,512]{1,0:T(8,128)(2,1)S(1)}, u32[]{:S(2)}, u32[]{:S(2)}) collective-permute-start(bf16[256,512]{1,0:T(8,128)(2,1)S(1)} %slice.90), channel_id=1, source_target_pairs={{0,1},{1,0},{2,3},{3,2},{4,5},{5,4},{6,7},{7,6},{8,9},{9,8},{10,11... | collective-permute-start | bytes 786440 | tf_op jit(solution)/shard_map/ppermute | solution.py:300
  208.3 9.3 %collective-permute-start.14 = (bf16[256,512]{1,0:T(8,128)(2,1)S(1)}, bf16[256,512]{1,0:T(8,128)(2,1)S(1)}, u32[]{:S(2)}, u32[]{:S(2)}) collective-permute-start(bf16[256,512]{1,0:T(8,128)(2,1)S(1)} %add.71), channel_id=1, source_target_pairs={{0,4},{1,5},{2,6},{3,7},{4,0},{5,1},{6,2},{7,3},{8,12},{9,13},{10,... | collective-permute-start | bytes 786440 | tf_op jit(solution)/shard_map/ppermute | solution.py:300
  210.2 35.7 %collective-permute-start.10 = (bf16[3,512,256]{1,2,0:T(8,128)(2,1)S(1)}, bf16[3,512,256]{1,2,0:T(8,128)(2,1)S(1)}, u32[]{:S(2)}, u32[]{:S(2)}) collective-permute-start(bf16[3,512,256]{1,2,0:T(8,128)(2,1)S(1)} %add.67), channel_id=1, source_target_pairs={{0,8},{1,9},{2,10},{3,11},{4,12},{5,13},{6,14},{7,15},{8,0},{9,1},... | collective-permute-start | bytes 2359304 | tf_op jit(solution)/shard_map/ppermute | solution.py:300
  211.1 36.3 %collective-permute-start.24 = (bf16[2,256,512]{2,1,0:T(8,128)(2,1)S(1)}, bf16[2,256,512]{2,1,0:T(8,128)(2,1)S(1)}, u32[]{:S(2)}, u32[]{:S(2)}) collective-permute-start(bf16[2,256,512]{2,1,0:T(8,128)(2,1)S(1)} %slice.96), channel_id=1, source_target_pairs={{0,8},{1,9},{2,3},{3,2},{4,12},{5,13},{6,7},{7,6},{8,0},{9,1},{10,... | collective-permute-start | bytes 1572872 | tf_op jit(solution)/shard_map/ppermute | solution.py:300
  217.7 26.3 %collective-permute-start.15 = (bf16[256,512]{1,0:T(8,128)(2,1)S(1)}, bf16[256,512]{1,0:T(8,128)(2,1)S(1)}, u32[]{:S(2)}, u32[]{:S(2)}) collective-permute-start(bf16[256,512]{1,0:T(8,128)(2,1)S(1)} %add.72), channel_id=1, source_target_pairs={{0,8},{1,9},{2,10},{3,11},{4,12},{5,13},{6,14},{7,15},{8,0},{9,1},... | collective-permute-start | bytes 786440 | tf_op jit(solution)/shard_map/ppermute | solution.py:300
  222.2 7.4 %collective-permute-start.18 = (f32[8,512]{1,0:T(8,128)S(1)}, f32[8,512]{1,0:T(8,128)S(1)}, u32[]{:S(2)}, u32[]{:S(2)}) collective-permute-start(f32[8,512]{1,0:T(8,128)S(1)} %add.75), channel_id=1, source_target_pairs={{0,2},{1,3},{2,0},{3,1},{4,6},{5,7},{6,4},{7,5},{8,10},{9,11},{10,... | collective-permute-start | bytes 49160 | tf_op jit(solution)/shard_map/ppermute | solution.py:300
  233.4 6.0 %collective-permute-start.20 = (f32[8,512]{1,0:T(8,128)S(1)}, f32[8,512]{1,0:T(8,128)S(1)}, u32[]{:S(2)}, u32[]{:S(2)}) collective-permute-start(f32[8,512]{1,0:T(8,128)S(1)} %add.77), channel_id=1, source_target_pairs={{0,8},{1,9},{2,10},{3,11},{4,12},{5,13},{6,14},{7,15},{8,0},{9,1},... | collective-permute-start | bytes 49160 | tf_op jit(solution)/shard_map/ppermute | solution.py:300
  239.4 4.6 %collective-permute-start.21 = (f32[8,512]{1,0:T(8,128)S(1)}, f32[8,512]{1,0:T(8,128)S(1)}, u32[]{:S(2)}, u32[]{:S(2)}) collective-permute-start(f32[8,512]{1,0:T(8,128)S(1)} %add.78), channel_id=1, source_target_pairs={{0,16},{1,17},{2,18},{3,19},{4,20},{5,21},{6,22},{7,23},{8,24},{9,... | collective-permute-start | bytes 49160 | tf_op jit(solution)/shard_map/ppermute | solution.py:300
  244.1 32.1 %collective-permute-start.16 = (bf16[256,512]{1,0:T(8,128)(2,1)S(1)}, bf16[256,512]{1,0:T(8,128)(2,1)S(1)}, u32[]{:S(2)}, u32[]{:S(2)}) collective-permute-start(bf16[256,512]{1,0:T(8,128)(2,1)S(1)} %add.73), channel_id=1, source_target_pairs={{0,16},{1,17},{2,18},{3,19},{4,20},{5,21},{6,22},{7,23},{8,24},{9,... | collective-permute-start | bytes 786440 | tf_op jit(solution)/shard_map/ppermute | solution.py:300
  246.1 49.8 %collective-permute-start.11 = (bf16[3,512,256]{1,2,0:T(8,128)(2,1)S(1)}, bf16[3,512,256]{1,2,0:T(8,128)(2,1)S(1)}, u32[]{:S(2)}, u32[]{:S(2)}) collective-permute-start(bf16[3,512,256]{1,2,0:T(8,128)(2,1)S(1)} %add.68), channel_id=1, source_target_pairs={{0,16},{1,17},{2,18},{3,19},{4,20},{5,21},{6,22},{7,23},{8,24},{9,... | collective-permute-start | bytes 2359304 | tf_op jit(solution)/shard_map/ppermute | solution.py:300
  247.5 29.6 %collective-permute-start.25 = (bf16[2,128,512]{2,1,0:T(8,128)(2,1)S(1)}, bf16[2,128,512]{2,1,0:T(8,128)(2,1)S(1)}, u32[]{:S(2)}, u32[]{:S(2)}) collective-permute-start(bf16[2,128,512]{2,1,0:T(8,128)(2,1)S(1)} %slice.98), channel_id=1, source_target_pairs={{0,4},{1,5},{2,10},{3,11},{4,0},{5,1},{6,14},{7,15},{8,12},{9,13},... | collective-permute-start | bytes 786440 | tf_op jit(solution)/shard_map/ppermute | solution.py:300
  277.1 22.0 %collective-permute-start.26 = (bf16[2,64,512]{2,1,0:T(8,128)(2,1)S(1)}, bf16[2,64,512]{2,1,0:T(8,128)(2,1)S(1)}, u32[]{:S(2)}, u32[]{:S(2)}) collective-permute-start(bf16[2,64,512]{2,1,0:T(8,128)(2,1)S(1)} %slice.100), channel_id=1, source_target_pairs={{0,16},{1,17},{2,18},{3,19},{4,20},{5,21},{6,22},{7,23},{8,24},{9,... | collective-permute-start | bytes 393224 | tf_op jit(solution)/shard_map/ppermute | solution.py:300
  (15 other events, 157.1 us)
